TPU v7x, 256 devices: a whole 4x4x8 slice. The times are simulated.
256 devices in a mesh: tile: 64 (over z, y, core), frame: 4 (over x).
Axes of the slice: x: 4, y: 4, z: 8, core: 2. Of those that a mesh axis runs over, the one named last changes fastest.
Arguments:
- movie: bfloat16 [1572864, 512], P('tile', 'frame'), may hold values from -150 to 150
- footprint: float32 [12288, 8, 128], P('tile'), may hold values from 0 to 1, as said below
- traces: float32 [12288, 512], P('tile', 'frame'), may hold values from 0.05 to 3
- slot_neuron: int32 [12288, 8], P('tile'), may hold values from 0 to 12288, as said below
- neuron_blocks: int32 [12288, 8], P('tile'), may hold values from 0 to 98304, as said below
Outputs:
- footprint_new: float32 [12288, 8, 128], P('tile', None, 'frame')
- traces_new: float32 [12288, 512], P('tile', 'frame')
Inputs may be any that keep to these rules, and one draw needn't show every extreme that they name: `slot_neuron`: entry 12288 marks an empty slot. Neuron n sits in exactly the slots that row n of neuron_blocks lists, at most once in a voxel block. `neuron_blocks`: row n lists the slot indices (voxel block * 8 + slot) of neuron n: 1 to 8 consecutive voxel blocks in one slot, in increasing order, then the pad 12288 * 8. Neuron n has its home at tile index n // 192 and lies wholly in tile (n // 192 + n) mod 64. The blocks of one home tile index's neurons in one tile number at most 24, and some pair of home and tile reaches 24. `footprint`: zero in empty slots.
All inputs are finite; a program needn't handle non-finite values.
Results may differ from a plain program's by a relative error of at most 0.0054.
Values may be sent and summed in bfloat16 or wider, within the bound.
No kernel may reach another device: no remote copies, remote signals or barrier semaphores. Data moves between devices by JAX's collectives and lax.ppermute only.
A program may use at most 64 MiB of HBM per device.

v0:
```python
import jax
import jax.numpy as jnp
from jax import lax
from jax.experimental import pallas as pl
from jax.experimental.pallas import tpu as pltpu
from jax.sharding import PartitionSpec as P

sparsity = 50.0
lane = 128
head = 32
f32, bf16 = jnp.float32, jnp.bfloat16
nn = (((1,), (0,)), ((), ()))
nt = (((1,), (1,)), ((), ()))


def dot(a, b, dims=nn):
    return lax.dot_general(a, b, dims, preferred_element_type=f32)


def halves(x):
    high = x.astype(bf16)
    return high, (x - high.astype(f32)).astype(bf16)


def masks():
    row = lax.broadcasted_iota(jnp.int32, (lane, lane), 0)
    col = lax.broadcasted_iota(jnp.int32, (lane, lane), 1)
    return row == col, (row // 8) == (col // 8)


def column(eye, row):
    return jnp.sum(jnp.where(eye, row, 0.0), axis=1, keepdims=True)


def residents(tile, homes, tiles, axis):
    shape = (1, 4 * tiles) if axis else (4 * tiles, 1)
    k = lax.broadcasted_iota(jnp.int32, shape, axis)
    home, j = lax.div(k, 4), lax.rem(k, 4)
    name = homes * home + tiles * j + lax.rem(tile + tiles - home, tiles)
    return jnp.where(j < homes // tiles, name, -1)


def load_kernel(movie_hbm, movie, sem):
    copy = pltpu.make_async_copy(movie_hbm.at[pl.ds(0, movie.shape[0])], movie, sem)
    copy.start()
    copy.wait()


def first_kernel(first, groups, held, voxels, homes, tiles, *refs):
    place, recv, owner, movie, foot_hbm, movie_hbm, rows, exact, packed, foot, piece, grams, sem_f, sem_m = refs
    foot_copy = pltpu.make_async_copy(foot_hbm.at[pl.ds(first * lane, groups * lane)], foot, sem_f)
    piece_copy = pltpu.make_async_copy(
        movie_hbm.at[pl.ds((first + held) * voxels, piece.shape[0])], piece, sem_m
    )
    foot_copy.start()
    piece_copy.start()
    eye, block = masks()
    names = residents(place[0], homes, tiles, 1).astype(f32)
    sources = recv[...]
    for g in range(groups):
        own = column(eye, owner[first + g : first + g + 1, :].astype(f32))
        rows[g * lane : (g + 1) * lane, :] = dot((own == names).astype(bf16), sources).astype(bf16)
    for g in range(groups):
        if g == held:
            piece_copy.wait()
        film, where = (movie, g * voxels) if g < held else (piece, (g - held) * voxels)
        for p in range(8):
            start = g * lane + p * 16
            both = dot(rows[start : start + 16, :], film[where + p * 256 : where + (p + 1) * 256, :], nt)
            exact[16 + start : 32 + start, :] = jnp.concatenate([both[:8, :lane], both[8:, lane:]], 0)
    diagonals = []
    for g in range(groups):
        at = slice(g * lane, (g + 1) * lane)
        gram = jnp.where(block, dot(rows[at, :], rows[at, :], nt), 0.0)
        diagonals.append(jnp.sum(jnp.where(eye, gram, 0.0), axis=0, keepdims=True))
        high, low = halves(gram)
        grams[at, :lane] = high
        grams[at, lane:] = low
    diagonal = jnp.concatenate(diagonals + [jnp.zeros((16 - groups, lane), f32)], 0)
    exact[0:16, :] = diagonal
    high, low = halves(diagonal)
    packed[0:16, :] = high
    packed[16:32, :] = low
    foot_copy.wait()
    for g in range(groups):
        at = slice(g * lane, (g + 1) * lane)
        high, low = halves(foot[at, :])
        mixed = dot(grams[at, :], jnp.concatenate([high, high], 0)) + dot(grams[at, :lane], low)
        here = slice(16 + g * lane, 16 + (g + 1) * lane)
        part = exact[here, :] - mixed
        exact[here, :] = part
        packed[head + g * lane : head + (g + 1) * lane, :] = part.astype(bf16)
    if held == groups:
        piece_copy.wait()


def join_kernel(mine, got, exact, packed):
    diagonal = mine[0:16, :] + got[0:16, :].astype(f32) + got[16:32, :].astype(f32)
    exact[0:16, :] = diagonal
    high, low = halves(diagonal)
    packed[0:16, :] = high
    packed[16:32, :] = low
    rest = mine[16:, :] + got[head:, :].astype(f32)
    exact[16:, :] = rest
    packed[head:, :] = rest.astype(bf16)


def leaving_kernel(tile, traces, out, spread):
    tiles = out.shape[0] // 4
    for j in range(4):
        if j * tiles < traces.shape[0]:
            piece = pltpu.roll(traces[j * tiles : (j + 1) * tiles, :], tile[0], 0)
        else:
            piece = jnp.zeros((tiles, lane), f32)
        spread[pl.ds(j, tiles, stride=4), :] = piece
    out[...] = spread[...].astype(bf16)


def home_kernel(tile, back, traces, out, spread):
    tiles = back.shape[0] // 4
    spread[...] = back[...].astype(jnp.int32).astype(f32)
    unit = jnp.exp2(spread[pl.ds(3, tiles, stride=4), :])
    shift = lax.rem(tiles - tile[0], tiles)
    for j in range(traces.shape[0] // tiles):
        at = slice(j * tiles, (j + 1) * tiles)
        step = pltpu.roll(spread[pl.ds(j, tiles, stride=4), :] * unit, shift, 0)
        out[at, :] = jnp.maximum(traces[at, :] + step, 0.0)


def turn(updated, frame, turned):
    slots, width, _ = turned.shape
    blocks = updated.shape[0] // slots
    at_once = lane // width
    part = lax.broadcasted_iota(jnp.int32, (blocks, lane), 1) // width
    for first in range(0, slots, at_once):
        packed = jnp.zeros((blocks, lane), f32)
        for i in range(at_once):
            rows = updated[pl.ds(first + i, blocks, stride=slots), :]
            rows = pltpu.roll(rows, lax.rem(lane + (i - frame) * width, lane), 1)
            packed = jnp.where(part == i, rows, packed)
        packed = jnp.concatenate([packed, jnp.zeros((lane - blocks, lane), f32)], 0)
        turned[first : first + at_once, :, :] = packed.T.reshape(at_once, width, lane)


def join_turned(before, second, whole, blocks):
    after = pltpu.roll(second[...].reshape(-1, lane), blocks, 1)
    low = lax.broadcasted_iota(jnp.int32, after.shape, 1) < blocks
    both = jnp.where(low, before[...].reshape(-1, lane), after)
    whole[:, :, :lane] = both.reshape(before.shape)
    whole[:, :, lane:] = after.reshape(before.shape)[:, :, : whole.shape[2] - lane]


def second_kernel(first, groups, held, voxels, homes, tiles, begin, end, *refs):
    rest = list(refs)
    place, owner, rows, foot, movie, mine, got = [rest.pop(0) for _ in range(7)]
    piece = rest.pop(0) if held < groups else None
    before = None if begin else (rest.pop(0), rest.pop(0))
    turned_before = None if begin else rest.pop(0)
    turned = rest.pop(0)
    after = [rest.pop(0)] if end else [rest.pop(0), rest.pop(0)]
    updated, crosses, grads = rest[:3]
    eye, block = masks()
    low_rows = lax.broadcasted_iota(jnp.int32, (16, lane), 0) < 8
    owners = owner[first : first + groups, :]
    total = mine[0:16, :] + got[0:16, :].astype(f32) + got[16:32, :].astype(f32)
    inverse = jnp.where(owners < homes * tiles, 1.0 / total[:groups], 0.0)
    for g in range(groups):
        at = slice(g * lane, (g + 1) * lane)
        scale = column(eye, inverse[g : g + 1, :])
        residual = mine[16 + g * lane : 16 + (g + 1) * lane, :]
        residual += got[head + g * lane : head + (g + 1) * lane, :].astype(f32)
        new = jnp.maximum(foot[at, :] + (residual - sparsity) * scale, 0.0)
        new = jnp.where(scale > 0.0, new, 0.0)
        updated[at, :] = new
    if begin:
        turn(updated, place[1], turned)
    else:
        second, whole, sem_k = rest[3:]
        turn(updated, place[1], second)
        join_turned(turned_before, second, whole, first * lane // turned.shape[0])
        turned_copy = pltpu.make_async_copy(whole, turned, sem_k)
        turned_copy.start()
    norms = []
    for g in range(groups):
        at = slice(g * lane, (g + 1) * lane)
        high, low = halves(updated[at, :])
        cross = dot(jnp.concatenate([high, low], 1), jnp.concatenate([high, high], 1), nt) + dot(high, low, nt)
        cross = jnp.where(block, cross, 0.0)
        norms.append(jnp.sum(jnp.where(eye, cross, 0.0), axis=0, keepdims=True))
        high, low = halves(cross)
        crosses[at, :lane] = high
        crosses[at, lane:] = low
    for g in range(groups):
        at = slice(g * lane, (g + 1) * lane)
        known = dot(crosses[at, :], jnp.concatenate([rows[at, :], rows[at, :]], 0))
        film, where = (movie, g * voxels) if g < held else (piece, (g - held) * voxels)
        for p in range(8):
            two = slice(where + p * 256, where + (p + 1) * 256)
            part = updated[g * lane + 16 * p : g * lane + 16 * p + 16, :]
            wide = jnp.concatenate([jnp.where(low_rows, part, 0.0), jnp.where(low_rows, 0.0, part)], 1)
            grad = dot(wide.astype(bf16), film[two, :]) - known[16 * p : 16 * p + 16]
            high, low = halves(grad)
            start = g * 2 * lane + 16 * p
            grads[start : start + 16, :] = high
            grads[start + lane : start + lane + 16, :] = low
    names = residents(place[0], homes, tiles, 0)
    trace_grad = jnp.zeros(after[0].shape, f32) if begin else before[0][...]
    weight = jnp.zeros(after[0].shape, f32) if begin else before[1][...]
    for g in range(groups):
        picks = owners[g : g + 1, :] == names
        onehot = picks.astype(f32).astype(bf16)
        trace_grad += dot(jnp.concatenate([onehot, onehot], 1), grads[g * 2 * lane : (g + 1) * 2 * lane, :])
        weight += jnp.where(picks, norms[g], 0.0)
    if end:
        step = trace_grad / jnp.maximum(jnp.sum(weight, axis=1, keepdims=True), 1.0)
        largest = jnp.maximum(jnp.max(jnp.abs(step), axis=(0, 1), keepdims=True), 1e-30)
        power = jnp.ceil(jnp.log2(largest * (1.0 / 32700.0)))
        whole = jnp.round(step * jnp.exp2(-power))
        spare = lax.rem(lax.broadcasted_iota(jnp.int32, step.shape, 0), 4) == 3
        after[0][...] = jnp.where(spare, power, whole).astype(jnp.int32).astype(jnp.int16)
    else:
        after[0][...] = trace_grad
        after[1][...] = weight
    if not begin:
        turned_copy.wait()


def local(movie, footprint, traces, slot_neuron, neuron_blocks):
    tiles, shares = lax.axis_size("tile"), lax.axis_size("frame")
    blocks, slots, width = footprint.shape
    homes, frames = traces.shape
    per_pair = homes // tiles
    slot_total = blocks * slots
    groups = slot_total // lane
    tile = lax.axis_index("tile")
    frame = lax.axis_index("frame")

    anywhere = pl.BlockSpec(memory_space=pl.ANY)
    vmem = pl.BlockSpec(memory_space=pltpu.VMEM)
    params = pltpu.CompilerParams(vmem_limit_bytes=32 * 1024 * 1024)

    def call(kernel, *static, **kw):
        return pl.pallas_call(lambda *refs: kernel(*static, *refs), compiler_params=params, **kw)

    def near(x):
        return pltpu.with_memory_space_constraint(x, pltpu.VMEM)

    def far(x):
        return pltpu.with_memory_space_constraint(x, pltpu.HBM)

    here = jnp.stack([tile, frame]).astype(jnp.int32)
    smem = pl.BlockSpec(memory_space=pltpu.SMEM)
    leaving = call(
        leaving_kernel,
        out_shape=pltpu.HBM((4 * tiles, frames), bf16),
        in_specs=[smem, vmem],
        out_specs=vmem,
        scratch_shapes=[pltpu.VMEM((4 * tiles, frames), f32)],
    )(here, far(traces))
    recv = lax.all_to_all(leaving.reshape(tiles, 4, frames), "tile", 0, 0).reshape(4 * tiles, frames)

    owner = slot_neuron.reshape(groups, lane)
    foot = footprint.reshape(slot_total, width)

    voxels = movie.shape[0] // groups
    counts = [groups // 2, groups - groups // 2]
    firsts = [0, counts[0]]
    pieces = [counts[0], counts[1] - 1, 1]
    owner = near(owner)
    pairs = [[(s, s ^ 1) for s in range(shares)], [(s, shares - 1 - s) for s in range(shares)]]

    def exact_shape(c):
        return pltpu.VMEM((counts[c] * lane + 16, width), f32)

    def sent_shape(c):
        return pltpu.VMEM((counts[c] * lane + head, width), bf16)

    def film_shape(k):
        return pltpu.VMEM((pieces[k] * voxels, frames), bf16)

    film = call(
        load_kernel,
        out_shape=film_shape(0),
        in_specs=[anywhere],
        out_specs=vmem,
        scratch_shapes=[pltpu.SemaphoreType.DMA],
        cost_estimate=pl.CostEstimate(flops=0, bytes_accessed=2 * movie.size, transcendentals=0),
    )(far(movie))

    films, held, mine, got = [film], [], [], []
    for c in range(2):
        row, exact, sent, shapes, film = call(
            first_kernel,
            firsts[c],
            counts[c],
            pieces[c],
            voxels,
            homes,
            tiles,
            out_shape=(
                pltpu.VMEM((counts[c] * lane, frames), bf16),
                exact_shape(c),
                sent_shape(c),
                pltpu.VMEM((counts[c] * lane, width), f32),
                film_shape(c + 1),
            ),
            in_specs=[smem, vmem, vmem, vmem, anywhere, anywhere],
            out_specs=(vmem,) * 5,
            scratch_shapes=[pltpu.VMEM((counts[c] * lane, 2 * lane), bf16)] + [pltpu.SemaphoreType.DMA] * 2,
        )(here, recv, owner, near(films[c]), far(foot), far(movie))
        films.append(film)
        held.append([row, shapes])
        mine.append(exact)
        got.append(lax.ppermute(sent, "frame", pairs[c]))
    for c in range(2):
        mine[c], sent = call(
            join_kernel, out_shape=(exact_shape(c), sent_shape(c)), in_specs=[vmem] * 2, out_specs=(vmem,) * 2
        )(near(mine[c]), near(got[c]))
        got[c] = lax.ppermute(sent, "frame", pairs[1 - c])

    kept, running = None, []
    for c in range(2):
        begin, end = c == 0, c == 1
        total_shape = (4 * tiles, frames)
        outs = [pltpu.VMEM((slots, width // shares, lane), f32)] if begin else [pltpu.HBM((slots, width // shares, blocks), f32)]
        outs += [pltpu.VMEM(total_shape, jnp.int16)] if end else [pltpu.VMEM(total_shape, f32)] * 2
        more = [] if begin else [
            pltpu.VMEM((slots, width // shares, lane), f32),
            pltpu.VMEM((slots, width // shares, blocks), f32),
            pltpu.SemaphoreType.DMA,
        ]
        old = [] if begin else [films[2]] + running + [kept]
        given = [*held[c], films[c], mine[c], got[c], *old]
        kept, *running = call(
            second_kernel,
            firsts[c],
            counts[c],
            pieces[c],
            voxels,
            homes,
            tiles,
            begin,
            end,
            out_shape=tuple(outs),
            in_specs=[smem] + [vmem] * (1 + len(given)),
            out_specs=(vmem if begin else anywhere,) + (vmem,) * (len(outs) - 1),
            scratch_shapes=[
                pltpu.VMEM((counts[c] * lane, width), f32),
                pltpu.VMEM((counts[c] * lane, 2 * lane), bf16),
                pltpu.VMEM((2 * counts[c] * lane, frames), bf16),
            ]
            + more,
        )(here, owner, *[near(x) for x in given])
    ratio = running[0]

    back = lax.all_to_all(ratio.reshape(tiles, 4, frames), "tile", 0, 0)
    traces_new = call(
        home_kernel,
        out_shape=jax.ShapeDtypeStruct(traces.shape, f32),
        in_specs=[smem, vmem, vmem],
        out_specs=vmem,
        scratch_shapes=[pltpu.VMEM((4 * tiles, frames), f32)],
    )(here, near(back.reshape(4 * tiles, frames)), near(traces))
    return kept.transpose(2, 0, 1), traces_new


def solution(mesh):
    return jax.shard_map(
        local,
        mesh=mesh,
        in_specs=(
            P("tile", "frame"),
            P("tile", None, None),
            P("tile", "frame"),
            P("tile", None),
            P("tile", None),
        ),
        out_specs=(P("tile", None, "frame"), P("tile", "frame")),
        check_vma=False,
    )
```

profile of v0, /device:TPU:1, one launch (start us, length us, event | category | flops | bytes accessed | tf_op | source)
XLA Modules:
  0.0 64.9 jit_solution(2568041151314219186)
XLA Ops:
  0.6 0.1 pad_add_fusion.refs_0_
  0.7 1.6 %shard_map.59 = bf16[256,128]{1,0:T(8,128)(2,1)} custom-call(s32[2]{0:T(128)S(1)} %pad_add_fusion.refs_0_, f32[192,128]{1,0:T(8,128)} %refs_2_.1), custom_call_target="tpu_custom_call" | custom-call | tf_op jit(solution)/shard_map/pallas_call | solution.py:253
  2.3 13.2 %all-to-all-start = ((bf16[64,4,128]{2,1,0:T(4,128)(2,1)}), bf16[64,4,128]{2,1,0:T(4,128)(2,1)S(1)}, u32[]{:S(2)}, u32[]{:S(2)}) async-start(bf16[64,4,128]{2,1,0:T(4,128)(2,1)} %bitcast.14), calls=%async_computation | async-start | bytes 131072 | tf_op jit(solution)/shard_map/all_to_all | solution.py:260
  15.4 0.8 %copy.7 = s32[192,8]{1,0:T(8,128)S(1)} copy(s32[192,8]{0,1:T(8,128)} %param.8) | data formatting | bytes 12288 | tf_op args[3]
  16.2 0.1 reshape.22.refs_2_.refs_1_
  16.4 1.9 %shard_map.60.refs_3_.refs_4_ = bf16[12288,128]{1,0:T(8,128)(2,1)S(1)} custom-call(bf16[24576,128]{1,0:T(8,128)(2,1)} %refs_5_.3), custom_call_target="tpu_custom_call" | custom-call | bytes 6291456 | tf_op jit(solution)/shard_map/pallas_call | solution.py:281
  18.3 7.3 %all-to-all-done = bf16[64,4,128]{2,1,0:T(4,128)(2,1)S(1)} async-done(((bf16[64,4,128]{2,1,0:T(4,128)(2,1)}), bf16[64,4,128]{2,1,0:T(4,128)(2,1)S(1)}, u32[]{:S(2)}, u32[]{:S(2)}) %all-to-all-start) | async-done | bytes 65568 | tf_op jit(solution)/shard_map/all_to_all | solution.py:260
  25.5 2.4 %shard_map.61 = (bf16[768,128]{1,0:T(8,128)(2,1)S(1)}, f32[784,128]{1,0:T(8,128)S(1)}, bf16[800,128]{1,0:T(8,128)(2,1)S(1)}, f32[768,128]{1,0:T(8,128)S(1)}, bf16[10240,128]{1,0:T(8,128)(2,1)S(1)}) custom-call(s32[2]{0:T(128)S(1)} %pad_add_fusion.refs_0_, bf16[256,128]{1,0:T(8,128)(2,1)S(1)} %bitcast.8, s32[12,128]{1,0:T(8,128)S(1)} %reshape.22.refs_2_.refs_1_, ...), custom_call_target="tpu_custom_call" | custom-call | tf_op jit(solution)/shard_map/pallas_call | solution.py:292
  28.0 1.3 %collective-permute-start.2 = (bf16[800,128]{1,0:T(8,128)(2,1)S(1)}, bf16[800,128]{1,0:T(8,128)(2,1)S(1)}, u32[]{:S(2)}, u32[]{:S(2)}) collective-permute-start(bf16[800,128]{1,0:T(8,128)(2,1)S(1)} %get-tuple-element.32), channel_id=1, source_target_pairs={{0,1},{1,0},{2,3},{3,2},{4,5},{5,4},{6,7},{7,6},{8,9},{9,8},{10,11... | collective-permute-start | bytes 614408 | tf_op jit(solution)/shard_map/ppermute | solution.py:314
  29.3 2.5 %shard_map.62 = (bf16[768,128]{1,0:T(8,128)(2,1)S(1)}, f32[784,128]{1,0:T(8,128)S(1)}, bf16[800,128]{1,0:T(8,128)(2,1)S(1)}, f32[768,128]{1,0:T(8,128)S(1)}, bf16[2048,128]{1,0:T(8,128)(2,1)S(1)}) custom-call(s32[2]{0:T(128)S(1)} %pad_add_fusion.refs_0_, bf16[256,128]{1,0:T(8,128)(2,1)S(1)} %bitcast.9, s32[12,128]{1,0:T(8,128)S(1)} %reshape.22.refs_2_.refs_1_, ...), custom_call_target="tpu_custom_call" | custom-call | tf_op jit(solution)/shard_map/pallas_call | solution.py:292
  31.8 1.9 %collective-permute-start = (bf16[800,128]{1,0:T(8,128)(2,1)S(1)}, bf16[800,128]{1,0:T(8,128)(2,1)S(1)}, u32[]{:S(2)}, u32[]{:S(2)}) collective-permute-start(bf16[800,128]{1,0:T(8,128)(2,1)S(1)} %get-tuple-element.25), channel_id=1, source_target_pairs={{0,3},{1,2},{2,1},{3,0},{4,7},{5,6},{6,5},{7,4},{8,11},{9,10},{10,... | collective-permute-start | bytes 614408 | tf_op jit(solution)/shard_map/ppermute | solution.py:314
  33.7 0.7 %collective-permute-done.2.refs_1_ = bf16[800,128]{1,0:T(8,128)(2,1)S(1)} collective-permute-done((bf16[800,128]{1,0:T(8,128)(2,1)S(1)}, bf16[800,128]{1,0:T(8,128)(2,1)S(1)}, u32[]{:S(2)}, u32[]{:S(2)}) %collective-permute-start.2) | collective-permute-done | bytes 204832 | tf_op jit(solution)/shard_map/ppermute | solution.py:314
  34.3 0.1 shard_map.64
  34.4 2.6 %collective-permute-start.3 = (bf16[800,128]{1,0:T(8,128)(2,1)S(1)}, bf16[800,128]{1,0:T(8,128)(2,1)S(1)}, u32[]{:S(2)}, u32[]{:S(2)}) collective-permute-start(bf16[800,128]{1,0:T(8,128)(2,1)S(1)} %get-tuple-element.34), channel_id=1, source_target_pairs={{0,3},{1,2},{2,1},{3,0},{4,7},{5,6},{6,5},{7,4},{8,11},{9,10},{10,... | collective-permute-start | bytes 614408 | tf_op jit(solution)/shard_map/ppermute | solution.py:319
  36.9 2.1 %collective-permute-done.refs_1_ = bf16[800,128]{1,0:T(8,128)(2,1)S(1)} collective-permute-done((bf16[800,128]{1,0:T(8,128)(2,1)S(1)}, bf16[800,128]{1,0:T(8,128)(2,1)S(1)}, u32[]{:S(2)}, u32[]{:S(2)}) %collective-permute-start) | collective-permute-done | bytes 204832 | tf_op jit(solution)/shard_map/ppermute | solution.py:314
  39.0 0.1 shard_map.63
  39.1 0.1 collective-permute-start.1
  39.2 4.2 %collective-permute-done.3.refs_6_ = bf16[800,128]{1,0:T(8,128)(2,1)S(1)} collective-permute-done((bf16[800,128]{1,0:T(8,128)(2,1)S(1)}, bf16[800,128]{1,0:T(8,128)(2,1)S(1)}, u32[]{:S(2)}, u32[]{:S(2)}) %collective-permute-start.3) | collective-permute-done | bytes 204832 | tf_op jit(solution)/shard_map/ppermute | solution.py:319
  43.4 1.8 %shard_map.65 = (f32[8,32,128]{2,1,0:T(8,128)S(1)}, f32[256,128]{1,0:T(8,128)S(1)}, f32[256,128]{1,0:T(8,128)S(1)}) custom-call(s32[2]{0:T(128)S(1)} %pad_add_fusion.refs_0_, s32[12,128]{1,0:T(8,128)S(1)} %reshape.22.refs_2_.refs_1_, bf16[768,128]{1,0:T(8,128)(2,1)S(1)} %get-tuple-element.29.refs_2_, f32[768,128]{1,0:T(8,128)S(1)} %get-tuple-element.30.refs_3_, ...), custom_call_target="tpu_custom_call" | custom-call | tf_op jit(solution)/shard_map/pallas_call | solution.py:334
  45.2 0.0 copy-start
  45.2 0.0 collective-permute-done.1.refs_6_
  45.2 2.7 %shard_map.66 = (f32[8,32,192]{2,1,0:T(8,128)}, s16[256,128]{1,0:T(8,128)(2,1)S(1)}) custom-call(s32[2]{0:T(128)S(1)} %pad_add_fusion.refs_0_, s32[12,128]{1,0:T(8,128)S(1)} %reshape.22.refs_2_.refs_1_, bf16[768,128]{1,0:T(8,128)(2,1)S(1)} %get-tuple-element.22.refs_2_, f32[768,128]{1,0:T(8,128)S(1)} %get-tuple-element.23.refs_3_, ...), custom_call_target="tpu_custom_call" | custom-call | tf_op jit(solution)/shard_map/pallas_call | solution.py:334
  47.9 15.7 %all_to_all.10 = s16[64,4,128]{2,1,0:T(4,128)(2,1)S(1)} all-to-all(s16[64,4,128]{2,1,0:T(4,128)(2,1)S(1)} %bitcast.11), channel_id=1, replica_groups=mesh['tile'=64,'frame'=4] {'tile'}, dimensions={0} | all-to-all | bytes 131072 | tf_op jit(solution)/shard_map/all_to_all | solution.py:356
  63.7 1.2 %shard_map.67 = f32[192,128]{1,0:T(8,128)} custom-call(s32[2]{0:T(128)S(1)} %pad_add_fusion.refs_0_, s16[256,128]{1,0:T(8,128)(2,1)S(1)} %bitcast.10, f32[192,128]{1,0:T(8,128)S(1)} %copy-done), custom_call_target="tpu_custom_call" | custom-call | tf_op jit(solution)/shard_map/pallas_call | solution.py:357
  (1 shorter events, 0.0 us)
Async XLA Ops:
  2.3 23.3 %all-to-all-start = ((bf16[64,4,128]{2,1,0:T(4,128)(2,1)}), bf16[64,4,128]{2,1,0:T(4,128)(2,1)S(1)}, u32[]{:S(2)}, u32[]{:S(2)}) async-start(bf16[64,4,128]{2,1,0:T(4,128)(2,1)} %bitcast.14), calls=%async_computation | async-start | bytes 131072 | tf_op jit(solution)/shard_map/all_to_all | solution.py:260
  28.0 6.4 %collective-permute-start.2 = (bf16[800,128]{1,0:T(8,128)(2,1)S(1)}, bf16[800,128]{1,0:T(8,128)(2,1)S(1)}, u32[]{:S(2)}, u32[]{:S(2)}) collective-permute-start(bf16[800,128]{1,0:T(8,128)(2,1)S(1)} %get-tuple-element.32), channel_id=1, source_target_pairs={{0,1},{1,0},{2,3},{3,2},{4,5},{5,4},{6,7},{7,6},{8,9},{9,8},{10,11... | collective-permute-start | bytes 614408 | tf_op jit(solution)/shard_map/ppermute | solution.py:314
  31.8 7.2 %collective-permute-start = (bf16[800,128]{1,0:T(8,128)(2,1)S(1)}, bf16[800,128]{1,0:T(8,128)(2,1)S(1)}, u32[]{:S(2)}, u32[]{:S(2)}) collective-permute-start(bf16[800,128]{1,0:T(8,128)(2,1)S(1)} %get-tuple-element.25), channel_id=1, source_target_pairs={{0,3},{1,2},{2,1},{3,0},{4,7},{5,6},{6,5},{7,4},{8,11},{9,10},{10,... | collective-permute-start | bytes 614408 | tf_op jit(solution)/shard_map/ppermute | solution.py:314
  34.4 9.0 %collective-permute-start.3 = (bf16[800,128]{1,0:T(8,128)(2,1)S(1)}, bf16[800,128]{1,0:T(8,128)(2,1)S(1)}, u32[]{:S(2)}, u32[]{:S(2)}) collective-permute-start(bf16[800,128]{1,0:T(8,128)(2,1)S(1)} %get-tuple-element.34), channel_id=1, source_target_pairs={{0,3},{1,2},{2,1},{3,0},{4,7},{5,6},{6,5},{7,4},{8,11},{9,10},{10,... | collective-permute-start | bytes 614408 | tf_op jit(solution)/shard_map/ppermute | solution.py:319
  39.1 6.2 %collective-permute-start.1 = (bf16[800,128]{1,0:T(8,128)(2,1)S(1)}, bf16[800,128]{1,0:T(8,128)(2,1)S(1)}, u32[]{:S(2)}, u32[]{:S(2)}) collective-permute-start(bf16[800,128]{1,0:T(8,128)(2,1)S(1)} %get-tuple-element.27), channel_id=1, source_target_pairs={{0,1},{1,0},{2,3},{3,2},{4,5},{5,4},{6,7},{7,6},{8,9},{9,8},{10,11... | collective-permute-start | bytes 614408 | tf_op jit(solution)/shard_map/ppermute | solution.py:319
  45.2 18.4 %copy-start = (f32[192,128]{1,0:T(8,128)S(1)}, f32[192,128]{1,0:T(8,128)}, u32[]{:S(2)}) copy-start(f32[192,128]{1,0:T(8,128)} %refs_2_.1) | copy-start | bytes 294916
where the time goes:
time: 65.2 us; the launch traced here: 64.9 us
  starting transfers between devices  19 us (29%)
  blocking collectives  15.7 us (24%)
  Pallas kernels  14.2 us (22%)
  waiting for transfers between devices  14.2 us (22%)
  local copies, waits for them, and re-layouts  0.91 us (1%)
  between operations  0.73 us (1%)
    all_to_all x1, blocking collectives, local(): back = lax.all_to_all(ratio.reshape(tiles, 4, frames), 'tile', 0, 0)  15.7 us
    all_to_all x1, starting transfers between devices, local(): lax.all_to_all(leaving.reshape(tiles, 4, frames), 'tile', 0, 0)  13.2 us
    all_to_all x1, waiting for transfers between devices, local(): lax.all_to_all(leaving.reshape(tiles, 4, frames), 'tile', 0, 0)  7.26 us
    pallas_call x2, Pallas kernels, local(): call(first_kernel, firsts[c], counts[c], pieces[c], voxels, homes, tiles,...  4.93 us
    pallas_call x2, Pallas kernels, local(): call(second_kernel, firsts[c], counts[c], pieces[c], voxels, homes, tiles...  4.5 us
    ppermute x2, waiting for transfers between devices, local(): got[c] = lax.ppermute(sent, 'frame', pairs[1 - c])  4.23 us
    ppermute x2, starting transfers between devices, local(): got.append(lax.ppermute(sent, 'frame', pairs[c]))  3.2 us
    ppermute x2, waiting for transfers between devices, local(): got.append(lax.ppermute(sent, 'frame', pairs[c]))  2.72 us
  transfers between devices with their start and end apart: 5, of which 4 were waited for; matrix products, arithmetic and copies ran while one was open for 1% of the time, Pallas kernels for 10%

commit v1 on v0

--- a/solution.py
+++ b/solution.py
@@ -40,22 +40,40 @@
     return jnp.where(j < homes // tiles, name, -1)
 
 
-def load_kernel(movie_hbm, movie, sem):
+def load_kernel(by_slot_hbm, movie_hbm, movie, owner, by_slot, sem, sem_s):
+    slot_copy = pltpu.make_async_copy(by_slot_hbm, by_slot, sem_s)
     copy = pltpu.make_async_copy(movie_hbm.at[pl.ds(0, movie.shape[0])], movie, sem)
+    slot_copy.start()
     copy.start()
+    slots, blocks = by_slot.shape
+    block = lax.broadcasted_iota(jnp.int32, (blocks, lane), 0)
+    place = lax.broadcasted_iota(jnp.int32, (blocks, lane), 1)
+    mine = lax.broadcasted_iota(jnp.int32, (slots, lane), 1) % slots
+    mine = mine == lax.broadcasted_iota(jnp.int32, (slots, lane), 0)
+    slot_copy.wait()
+    names = by_slot[...]
+    high = (names // 128).astype(f32).astype(bf16)
+    low = (names % 128).astype(f32).astype(bf16)
+    both = jnp.concatenate([high, low], 0)
+    for g in range(owner.shape[0]):
+        pick = (block == g * (lane // slots) + place // slots).astype(f32).astype(bf16)
+        wide = dot(both, pick)
+        wide = wide[:slots] * 128.0 + wide[slots:]
+        row = jnp.sum(jnp.where(mine, wide, 0.0), axis=0, keepdims=True)
+        owner[g : g + 1, :] = row.astype(jnp.int32)
     copy.wait()
 
 
 def first_kernel(first, groups, held, voxels, homes, tiles, *refs):
-    place, recv, owner, movie, foot_hbm, movie_hbm, rows, exact, packed, foot, piece, grams, sem_f, sem_m = refs
+    recv, owner, movie, foot_hbm, movie_hbm, rows, exact, packed, foot, piece, grams, sem_f, sem_m = refs
     foot_copy = pltpu.make_async_copy(foot_hbm.at[pl.ds(first * lane, groups * lane)], foot, sem_f)
     piece_copy = pltpu.make_async_copy(
         movie_hbm.at[pl.ds((first + held) * voxels, piece.shape[0])], piece, sem_m
     )
-    foot_copy.start()
-    piece_copy.start()
+    for copy in (foot_copy, piece_copy) if held == groups else (piece_copy, foot_copy):
+        copy.start()
     eye, block = masks()
-    names = residents(place[0], homes, tiles, 1).astype(f32)
+    names = residents(lax.axis_index("tile"), homes, tiles, 1).astype(f32)
     sources = recv[...]
     for g in range(groups):
         own = column(eye, owner[first + g : first + g + 1, :].astype(f32))
@@ -105,26 +123,32 @@
     packed[head:, :] = rest.astype(bf16)
 
 
-def leaving_kernel(tile, traces, out, spread):
+def leaving_kernel(traces, out, spread):
     tiles = out.shape[0] // 4
     for j in range(4):
         if j * tiles < traces.shape[0]:
-            piece = pltpu.roll(traces[j * tiles : (j + 1) * tiles, :], tile[0], 0)
+            piece = pltpu.roll(traces[j * tiles : (j + 1) * tiles, :], lax.axis_index("tile"), 0)
         else:
             piece = jnp.zeros((tiles, lane), f32)
         spread[pl.ds(j, tiles, stride=4), :] = piece
     out[...] = spread[...].astype(bf16)
 
 
-def home_kernel(tile, back, traces, out, spread):
+def home_kernel(back, traces, turned, out_hbm, turned_hbm, spread, out, sem_t, sem_o):
+    turned_copy = pltpu.make_async_copy(turned, turned_hbm, sem_t)
+    turned_copy.start()
     tiles = back.shape[0] // 4
     spread[...] = back[...].astype(jnp.int32).astype(f32)
     unit = jnp.exp2(spread[pl.ds(3, tiles, stride=4), :])
-    shift = lax.rem(tiles - tile[0], tiles)
+    shift = lax.rem(tiles - lax.axis_index("tile"), tiles)
     for j in range(traces.shape[0] // tiles):
         at = slice(j * tiles, (j + 1) * tiles)
         step = pltpu.roll(spread[pl.ds(j, tiles, stride=4), :] * unit, shift, 0)
         out[at, :] = jnp.maximum(traces[at, :] + step, 0.0)
+    out_copy = pltpu.make_async_copy(out, out_hbm, sem_o)
+    out_copy.start()
+    turned_copy.wait()
+    out_copy.wait()
 
 
 def turn(updated, frame, turned):
@@ -152,7 +176,7 @@
 
 def second_kernel(first, groups, held, voxels, homes, tiles, begin, end, *refs):
     rest = list(refs)
-    place, owner, rows, foot, movie, mine, got = [rest.pop(0) for _ in range(7)]
+    owner, rows, foot, movie, mine, got = [rest.pop(0) for _ in range(6)]
     piece = rest.pop(0) if held < groups else None
     before = None if begin else (rest.pop(0), rest.pop(0))
     turned_before = None if begin else rest.pop(0)
@@ -173,13 +197,11 @@
         new = jnp.where(scale > 0.0, new, 0.0)
         updated[at, :] = new
     if begin:
-        turn(updated, place[1], turned)
+        turn(updated, lax.axis_index("frame"), turned)
     else:
-        second, whole, sem_k = rest[3:]
-        turn(updated, place[1], second)
-        join_turned(turned_before, second, whole, first * lane // turned.shape[0])
-        turned_copy = pltpu.make_async_copy(whole, turned, sem_k)
-        turned_copy.start()
+        second = rest[3]
+        turn(updated, lax.axis_index("frame"), second)
+        join_turned(turned_before, second, turned, first * lane // turned.shape[0])
     norms = []
     for g in range(groups):
         at = slice(g * lane, (g + 1) * lane)
@@ -203,7 +225,7 @@
             start = g * 2 * lane + 16 * p
             grads[start : start + 16, :] = high
             grads[start + lane : start + lane + 16, :] = low
-    names = residents(place[0], homes, tiles, 0)
+    names = residents(lax.axis_index("tile"), homes, tiles, 0)
     trace_grad = jnp.zeros(after[0].shape, f32) if begin else before[0][...]
     weight = jnp.zeros(after[0].shape, f32) if begin else before[1][...]
     for g in range(groups):
@@ -221,8 +243,6 @@
     else:
         after[0][...] = trace_grad
         after[1][...] = weight
-    if not begin:
-        turned_copy.wait()
 
 
 def local(movie, footprint, traces, slot_neuron, neuron_blocks):
@@ -232,8 +252,6 @@
     per_pair = homes // tiles
     slot_total = blocks * slots
     groups = slot_total // lane
-    tile = lax.axis_index("tile")
-    frame = lax.axis_index("frame")
 
     anywhere = pl.BlockSpec(memory_space=pl.ANY)
     vmem = pl.BlockSpec(memory_space=pltpu.VMEM)
@@ -248,25 +266,21 @@
     def far(x):
         return pltpu.with_memory_space_constraint(x, pltpu.HBM)
 
-    here = jnp.stack([tile, frame]).astype(jnp.int32)
-    smem = pl.BlockSpec(memory_space=pltpu.SMEM)
     leaving = call(
         leaving_kernel,
         out_shape=pltpu.HBM((4 * tiles, frames), bf16),
-        in_specs=[smem, vmem],
+        in_specs=[vmem],
         out_specs=vmem,
         scratch_shapes=[pltpu.VMEM((4 * tiles, frames), f32)],
-    )(here, far(traces))
+    )(far(traces))
     recv = lax.all_to_all(leaving.reshape(tiles, 4, frames), "tile", 0, 0).reshape(4 * tiles, frames)
 
-    owner = slot_neuron.reshape(groups, lane)
     foot = footprint.reshape(slot_total, width)
 
     voxels = movie.shape[0] // groups
     counts = [groups // 2, groups - groups // 2]
     firsts = [0, counts[0]]
     pieces = [counts[0], counts[1] - 1, 1]
-    owner = near(owner)
     pairs = [[(s, s ^ 1) for s in range(shares)], [(s, shares - 1 - s) for s in range(shares)]]
 
     def exact_shape(c):
@@ -278,14 +292,15 @@
     def film_shape(k):
         return pltpu.VMEM((pieces[k] * voxels, frames), bf16)
 
-    film = call(
+    film, owner = call(
         load_kernel,
-        out_shape=film_shape(0),
-        in_specs=[anywhere],
-        out_specs=vmem,
-        scratch_shapes=[pltpu.SemaphoreType.DMA],
+        out_shape=(film_shape(0), pltpu.VMEM((groups, lane), jnp.int32)),
+        in_specs=[anywhere, anywhere],
+        out_specs=(vmem, vmem),
+        scratch_shapes=[pltpu.VMEM((slots, blocks), jnp.int32), pltpu.SemaphoreType.DMA, pltpu.SemaphoreType.DMA],
         cost_estimate=pl.CostEstimate(flops=0, bytes_accessed=2 * movie.size, transcendentals=0),
-    )(far(movie))
+    )(far(slot_neuron.T), far(movie))
+    owner = near(owner)
 
     films, held, mine, got = [film], [], [], []
     for c in range(2):
@@ -304,10 +319,10 @@
                 pltpu.VMEM((counts[c] * lane, width), f32),
                 film_shape(c + 1),
             ),
-            in_specs=[smem, vmem, vmem, vmem, anywhere, anywhere],
+            in_specs=[vmem, vmem, vmem, anywhere, anywhere],
             out_specs=(vmem,) * 5,
             scratch_shapes=[pltpu.VMEM((counts[c] * lane, 2 * lane), bf16)] + [pltpu.SemaphoreType.DMA] * 2,
-        )(here, recv, owner, near(films[c]), far(foot), far(movie))
+        )(recv, owner, near(films[c]), far(foot), far(movie))
         films.append(film)
         held.append([row, shapes])
         mine.append(exact)
@@ -322,13 +337,9 @@
     for c in range(2):
         begin, end = c == 0, c == 1
         total_shape = (4 * tiles, frames)
-        outs = [pltpu.VMEM((slots, width // shares, lane), f32)] if begin else [pltpu.HBM((slots, width // shares, blocks), f32)]
+        outs = [pltpu.VMEM((slots, width // shares, lane if begin else blocks), f32)]
         outs += [pltpu.VMEM(total_shape, jnp.int16)] if end else [pltpu.VMEM(total_shape, f32)] * 2
-        more = [] if begin else [
-            pltpu.VMEM((slots, width // shares, lane), f32),
-            pltpu.VMEM((slots, width // shares, blocks), f32),
-            pltpu.SemaphoreType.DMA,
-        ]
+        more = [] if begin else [pltpu.VMEM((slots, width // shares, lane), f32)]
         old = [] if begin else [films[2]] + running + [kept]
         given = [*held[c], films[c], mine[c], got[c], *old]
         kept, *running = call(
@@ -342,25 +353,30 @@
             begin,
             end,
             out_shape=tuple(outs),
-            in_specs=[smem] + [vmem] * (1 + len(given)),
-            out_specs=(vmem if begin else anywhere,) + (vmem,) * (len(outs) - 1),
+            in_specs=[vmem] * (1 + len(given)),
+            out_specs=(vmem,) * len(outs),
             scratch_shapes=[
                 pltpu.VMEM((counts[c] * lane, width), f32),
                 pltpu.VMEM((counts[c] * lane, 2 * lane), bf16),
                 pltpu.VMEM((2 * counts[c] * lane, frames), bf16),
             ]
             + more,
-        )(here, owner, *[near(x) for x in given])
+        )(owner, *[near(x) for x in given])
     ratio = running[0]
 
     back = lax.all_to_all(ratio.reshape(tiles, 4, frames), "tile", 0, 0)
-    traces_new = call(
+    traces_new, kept = call(
         home_kernel,
-        out_shape=jax.ShapeDtypeStruct(traces.shape, f32),
-        in_specs=[smem, vmem, vmem],
-        out_specs=vmem,
-        scratch_shapes=[pltpu.VMEM((4 * tiles, frames), f32)],
-    )(here, near(back.reshape(4 * tiles, frames)), near(traces))
+        out_shape=(pltpu.HBM(traces.shape, f32), pltpu.HBM(kept.shape, f32)),
+        in_specs=[vmem, vmem, vmem],
+        out_specs=(anywhere, anywhere),
+        scratch_shapes=[
+            pltpu.VMEM((4 * tiles, frames), f32),
+            pltpu.VMEM(traces.shape, f32),
+            pltpu.SemaphoreType.DMA,
+            pltpu.SemaphoreType.DMA,
+        ],
+    )(near(back.reshape(4 * tiles, frames)), near(traces), near(kept))
     return kept.transpose(2, 0, 1), traces_new
 
 

time: 65.2 us -> 62.1 us (0.952)
  Pallas kernels: 14.2 us -> 10.8 us
  waiting for transfers between devices: 14.2 us -> 15.2 us
  local copies, waits for them, and re-layouts: 0.91 us -> 0.01 us
    pallas_call x2, Pallas kernels: 4.5 us -> 2.75 us  [local(): call(second_kernel, firsts[c], counts[c], pieces[c], voxels, homes, tiles...]
    pallas_call x2, Pallas kernels: 4.93 us -> 3.74 us  [local(): call(first_kernel, firsts[c], counts[c], pieces[c], voxels, homes, tiles,...]
    all_to_all x1, waiting for transfers between devices: 7.26 us -> 8.15 us  [local(): lax.all_to_all(leaving.reshape(tiles, 4, frames), 'tile', 0, 0)]
    unnamed x3 -> x2, local copies, waits for them, and re-layouts: 0.81 us -> 0.01 us
  transfers between devices with their start and end apart: 5 -> 5, of which waited for: 4 -> 4; matrix products, arithmetic and copies ran while one was open for 1% -> 0% of each run, Pallas kernels for 10% -> 8%
where the time goes in v1:
time: 62.1 us; the launch traced here: 61.9 us
  starting transfers between devices  19 us (31%)
  blocking collectives  16.1 us (26%)
  waiting for transfers between devices  15.2 us (24%)
  Pallas kernels  10.8 us (17%)
  between operations  0.71 us (1%)
    all_to_all x1, blocking collectives, local(): back = lax.all_to_all(ratio.reshape(tiles, 4, frames), 'tile', 0, 0)  16.1 us
    all_to_all x1, starting transfers between devices, local(): lax.all_to_all(leaving.reshape(tiles, 4, frames), 'tile', 0, 0)  13.2 us
    all_to_all x1, waiting for transfers between devices, local(): lax.all_to_all(leaving.reshape(tiles, 4, frames), 'tile', 0, 0)  8.15 us
    ppermute x2, waiting for transfers between devices, local(): got[c] = lax.ppermute(sent, 'frame', pairs[1 - c])  4.33 us
    pallas_call x2, Pallas kernels, local(): call(first_kernel, firsts[c], counts[c], pieces[c], voxels, homes, tiles,...  3.74 us
    ppermute x2, starting transfers between devices, local(): got.append(lax.ppermute(sent, 'frame', pairs[c]))  3.2 us
    pallas_call x2, Pallas kernels, local(): call(second_kernel, firsts[c], counts[c], pieces[c], voxels, homes, tiles...  2.75 us
    ppermute x2, waiting for transfers between devices, local(): got.append(lax.ppermute(sent, 'frame', pairs[c]))  2.7 us
  transfers between devices with their start and end apart: 5, of which 4 were waited for; matrix products, arithmetic and copies ran while one was open for 0% of the time, Pallas kernels for 8%

profile of v1, /device:TPU:1, one launch (start us, length us, event | category | flops | bytes accessed | tf_op | source)
XLA Modules:
  0.0 61.9 jit_solution(10195895009317292970)
XLA Ops:
  0.6 1.6 %shard_map.60 = bf16[256,128]{1,0:T(8,128)(2,1)} custom-call(f32[192,128]{1,0:T(8,128)} %refs_1_.3), custom_call_target="tpu_custom_call" | custom-call | tf_op jit(solution)/shard_map/pallas_call | solution.py:269
  2.2 13.2 %all-to-all-start = ((bf16[64,4,128]{2,1,0:T(4,128)(2,1)}), bf16[64,4,128]{2,1,0:T(4,128)(2,1)S(1)}, u32[]{:S(2)}, u32[]{:S(2)}) async-start(bf16[64,4,128]{2,1,0:T(4,128)(2,1)} %bitcast.13), calls=%async_computation | async-start | bytes 131072 | tf_op jit(solution)/shard_map/all_to_all | solution.py:276
  15.4 1.9 %shard_map.59 = (bf16[12288,128]{1,0:T(8,128)(2,1)S(1)}, s32[12,128]{1,0:T(8,128)S(1)}) custom-call(s32[8,192]{1,0:T(8,128)} %bitcast.14, bf16[24576,128]{1,0:T(8,128)(2,1)} %refs_4_.3), custom_call_target="tpu_custom_call" | custom-call | bytes 6291456 | tf_op jit(solution)/shard_map/pallas_call | solution.py:295
  17.3 8.2 %all-to-all-done = bf16[64,4,128]{2,1,0:T(4,128)(2,1)S(1)} async-done(((bf16[64,4,128]{2,1,0:T(4,128)(2,1)}), bf16[64,4,128]{2,1,0:T(4,128)(2,1)S(1)}, u32[]{:S(2)}, u32[]{:S(2)}) %all-to-all-start) | async-done | bytes 65568 | tf_op jit(solution)/shard_map/all_to_all | solution.py:276
  25.4 1.9 %shard_map.61 = (bf16[768,128]{1,0:T(8,128)(2,1)S(1)}, f32[784,128]{1,0:T(8,128)S(1)}, bf16[800,128]{1,0:T(8,128)(2,1)S(1)}, f32[768,128]{1,0:T(8,128)S(1)}, bf16[10240,128]{1,0:T(8,128)(2,1)S(1)}) custom-call(bf16[256,128]{1,0:T(8,128)(2,1)S(1)} %bitcast.7, s32[12,128]{1,0:T(8,128)S(1)} %get-tuple-element.25.refs_1_.refs_0_, ...), custom_call_target="tpu_custom_call" | custom-call | tf_op jit(solution)/shard_map/pallas_call | solution.py:307
  27.4 1.3 %collective-permute-start.2 = (bf16[800,128]{1,0:T(8,128)(2,1)S(1)}, bf16[800,128]{1,0:T(8,128)(2,1)S(1)}, u32[]{:S(2)}, u32[]{:S(2)}) collective-permute-start(bf16[800,128]{1,0:T(8,128)(2,1)S(1)} %get-tuple-element.38), channel_id=1, source_target_pairs={{0,1},{1,0},{2,3},{3,2},{4,5},{5,4},{6,7},{7,6},{8,9},{9,8},{10,11... | collective-permute-start | bytes 614408 | tf_op jit(solution)/shard_map/ppermute | solution.py:329
  28.6 1.8 %shard_map.62 = (bf16[768,128]{1,0:T(8,128)(2,1)S(1)}, f32[784,128]{1,0:T(8,128)S(1)}, bf16[800,128]{1,0:T(8,128)(2,1)S(1)}, f32[768,128]{1,0:T(8,128)S(1)}, bf16[2048,128]{1,0:T(8,128)(2,1)S(1)}) custom-call(bf16[256,128]{1,0:T(8,128)(2,1)S(1)} %bitcast.8, s32[12,128]{1,0:T(8,128)S(1)} %get-tuple-element.25.refs_1_.refs_0_, ...), custom_call_target="tpu_custom_call" | custom-call | tf_op jit(solution)/shard_map/pallas_call | solution.py:307
  30.5 1.9 %collective-permute-start = (bf16[800,128]{1,0:T(8,128)(2,1)S(1)}, bf16[800,128]{1,0:T(8,128)(2,1)S(1)}, u32[]{:S(2)}, u32[]{:S(2)}) collective-permute-start(bf16[800,128]{1,0:T(8,128)(2,1)S(1)} %get-tuple-element.31), channel_id=1, source_target_pairs={{0,3},{1,2},{2,1},{3,0},{4,7},{5,6},{6,5},{7,4},{8,11},{9,10},{10,... | collective-permute-start | bytes 614408 | tf_op jit(solution)/shard_map/ppermute | solution.py:329
  32.4 1.3 %collective-permute-done.2.refs_1_ = bf16[800,128]{1,0:T(8,128)(2,1)S(1)} collective-permute-done((bf16[800,128]{1,0:T(8,128)(2,1)S(1)}, bf16[800,128]{1,0:T(8,128)(2,1)S(1)}, u32[]{:S(2)}, u32[]{:S(2)}) %collective-permute-start.2) | collective-permute-done | bytes 204832 | tf_op jit(solution)/shard_map/ppermute | solution.py:329
  33.7 0.1 shard_map.64
  33.8 2.6 %collective-permute-start.3 = (bf16[800,128]{1,0:T(8,128)(2,1)S(1)}, bf16[800,128]{1,0:T(8,128)(2,1)S(1)}, u32[]{:S(2)}, u32[]{:S(2)}) collective-permute-start(bf16[800,128]{1,0:T(8,128)(2,1)S(1)} %get-tuple-element.40), channel_id=1, source_target_pairs={{0,3},{1,2},{2,1},{3,0},{4,7},{5,6},{6,5},{7,4},{8,11},{9,10},{10,... | collective-permute-start | bytes 614408 | tf_op jit(solution)/shard_map/ppermute | solution.py:334
  36.3 1.4 %collective-permute-done.refs_1_ = bf16[800,128]{1,0:T(8,128)(2,1)S(1)} collective-permute-done((bf16[800,128]{1,0:T(8,128)(2,1)S(1)}, bf16[800,128]{1,0:T(8,128)(2,1)S(1)}, u32[]{:S(2)}, u32[]{:S(2)}) %collective-permute-start) | collective-permute-done | bytes 204832 | tf_op jit(solution)/shard_map/ppermute | solution.py:329
  37.7 0.1 shard_map.63
  37.8 0.1 collective-permute-start.1
  37.9 4.3 %collective-permute-done.3.refs_5_ = bf16[800,128]{1,0:T(8,128)(2,1)S(1)} collective-permute-done((bf16[800,128]{1,0:T(8,128)(2,1)S(1)}, bf16[800,128]{1,0:T(8,128)(2,1)S(1)}, u32[]{:S(2)}, u32[]{:S(2)}) %collective-permute-start.3) | collective-permute-done | bytes 204832 | tf_op jit(solution)/shard_map/ppermute | solution.py:334
  42.2 1.2 %shard_map.65 = (f32[8,32,128]{2,1,0:T(8,128)S(1)}, f32[256,128]{1,0:T(8,128)S(1)}, f32[256,128]{1,0:T(8,128)S(1)}) custom-call(s32[12,128]{1,0:T(8,128)S(1)} %get-tuple-element.25.refs_1_.refs_0_, bf16[768,128]{1,0:T(8,128)(2,1)S(1)} %get-tuple-element.35.refs_1_, f32[768,128]{1,0:T(8,128)S(1)} %get-tuple-element.36.refs_2_, ...), custom_call_target="tpu_custom_call" | custom-call | tf_op jit(solution)/shard_map/pallas_call | solution.py:345
  43.5 0.0 copy-start
  43.5 0.0 collective-permute-done.1.refs_5_
  43.5 1.5 %shard_map.66 = (f32[8,32,192]{2,1,0:T(8,128)S(1)}, s16[256,128]{1,0:T(8,128)(2,1)S(1)}) custom-call(s32[12,128]{1,0:T(8,128)S(1)} %get-tuple-element.25.refs_1_.refs_0_, bf16[768,128]{1,0:T(8,128)(2,1)S(1)} %get-tuple-element.28.refs_1_, f32[768,128]{1,0:T(8,128)S(1)} %get-tuple-element.29.refs_2_, ...), custom_call_target="tpu_custom_call" | custom-call | tf_op jit(solution)/shard_map/pallas_call | solution.py:345
  45.0 16.1 %all_to_all.10 = s16[64,4,128]{2,1,0:T(4,128)(2,1)S(1)} all-to-all(s16[64,4,128]{2,1,0:T(4,128)(2,1)S(1)} %bitcast.10), channel_id=1, replica_groups=mesh['tile'=64,'frame'=4] {'tile'}, dimensions={0} | all-to-all | bytes 131072 | tf_op jit(solution)/shard_map/all_to_all | solution.py:367
  61.1 0.0 copy-done
  61.1 0.7 %shard_map.67 = (f32[192,128]{1,0:T(8,128)}, f32[8,32,192]{2,1,0:T(8,128)}) custom-call(s16[256,128]{1,0:T(8,128)(2,1)S(1)} %bitcast.9, f32[192,128]{1,0:T(8,128)S(1)} %copy-done, f32[8,32,192]{2,1,0:T(8,128)S(1)} %get-tuple-element.45.refs_2_), custom_call_target="tpu_custom_call" | custom-call | tf_op jit(solution)/shard_map/pallas_call | solution.py:368
Async XLA Ops:
  2.2 23.3 %all-to-all-start = ((bf16[64,4,128]{2,1,0:T(4,128)(2,1)}), bf16[64,4,128]{2,1,0:T(4,128)(2,1)S(1)}, u32[]{:S(2)}, u32[]{:S(2)}) async-start(bf16[64,4,128]{2,1,0:T(4,128)(2,1)} %bitcast.13), calls=%async_computation | async-start | bytes 131072 | tf_op jit(solution)/shard_map/all_to_all | solution.py:276
  27.4 6.4 %collective-permute-start.2 = (bf16[800,128]{1,0:T(8,128)(2,1)S(1)}, bf16[800,128]{1,0:T(8,128)(2,1)S(1)}, u32[]{:S(2)}, u32[]{:S(2)}) collective-permute-start(bf16[800,128]{1,0:T(8,128)(2,1)S(1)} %get-tuple-element.38), channel_id=1, source_target_pairs={{0,1},{1,0},{2,3},{3,2},{4,5},{5,4},{6,7},{7,6},{8,9},{9,8},{10,11... | collective-permute-start | bytes 614408 | tf_op jit(solution)/shard_map/ppermute | solution.py:329
  30.5 7.2 %collective-permute-start = (bf16[800,128]{1,0:T(8,128)(2,1)S(1)}, bf16[800,128]{1,0:T(8,128)(2,1)S(1)}, u32[]{:S(2)}, u32[]{:S(2)}) collective-permute-start(bf16[800,128]{1,0:T(8,128)(2,1)S(1)} %get-tuple-element.31), channel_id=1, source_target_pairs={{0,3},{1,2},{2,1},{3,0},{4,7},{5,6},{6,5},{7,4},{8,11},{9,10},{10,... | collective-permute-start | bytes 614408 | tf_op jit(solution)/shard_map/ppermute | solution.py:329
  33.8 8.5 %collective-permute-start.3 = (bf16[800,128]{1,0:T(8,128)(2,1)S(1)}, bf16[800,128]{1,0:T(8,128)(2,1)S(1)}, u32[]{:S(2)}, u32[]{:S(2)}) collective-permute-start(bf16[800,128]{1,0:T(8,128)(2,1)S(1)} %get-tuple-element.40), channel_id=1, source_target_pairs={{0,3},{1,2},{2,1},{3,0},{4,7},{5,6},{6,5},{7,4},{8,11},{9,10},{10,... | collective-permute-start | bytes 614408 | tf_op jit(solution)/shard_map/ppermute | solution.py:334
  37.8 5.7 %collective-permute-start.1 = (bf16[800,128]{1,0:T(8,128)(2,1)S(1)}, bf16[800,128]{1,0:T(8,128)(2,1)S(1)}, u32[]{:S(2)}, u32[]{:S(2)}) collective-permute-start(bf16[800,128]{1,0:T(8,128)(2,1)S(1)} %get-tuple-element.33), channel_id=1, source_target_pairs={{0,1},{1,0},{2,3},{3,2},{4,5},{5,4},{6,7},{7,6},{8,9},{9,8},{10,11... | collective-permute-start | bytes 614408 | tf_op jit(solution)/shard_map/ppermute | solution.py:334
  43.5 17.7 %copy-start = (f32[192,128]{1,0:T(8,128)S(1)}, f32[192,128]{1,0:T(8,128)}, u32[]{:S(2)}) copy-start(f32[192,128]{1,0:T(8,128)} %refs_1_.3) | copy-start | bytes 294916
